TPU v7x, 32 devices: a whole 2x2x4 slice. The times are simulated.
32 devices in a mesh: dp: 8 (over y, x, core), seq: 4 (over z).
Axes of the slice: x: 2, y: 2, z: 4, core: 2. Of those that a mesh axis runs over, the one named last changes fastest.
Arguments:
- signal: bfloat16 [8, 2048, 1408], P('dp', 'seq'), may hold values from -240 to 240
- bases: int32 [8, 2048], P('dp', 'seq'), may hold values from 0 to 3
- base_table: bfloat16 [4, 1408], replicated, may hold values from -6 to 6
- conv_weight: bfloat16 [5, 1408, 1408], P(None, None, 'dp'), may hold values from -0.0625 to 0.0625
- batch_norm_gain: float32 [1408], replicated, may hold values from 0.1 to 1.9
- norm_bias: float32 [1408], replicated, may hold values from -3 to 3
- proj_weight: bfloat16 [1408, 1536], replicated, may hold values from -0.15625 to 0.15625
- attn_gain: float32 [1536], replicated, may hold values from 0.1 to 1.9
- q_weight: bfloat16 [1536, 1024], replicated, may hold values from -2 to 2
- k_weight: bfloat16 [1536, 128], replicated, may hold values from -2 to 2
- v_weight: bfloat16 [1536, 128], replicated, may hold values from -0.15625 to 0.15625
- bias_table: float32 [8, 32, 32], replicated, may hold values from -8 to 8
- buckets: int32 [8, 512], P('dp', 'seq'), may hold values from 0 to 31
- out_weight: bfloat16 [1024, 1536], replicated, may hold values from -1 to 1
Outputs:
- tokens: bfloat16 [8, 512, 1536], P('dp', 'seq')
- mixed: bfloat16 [8, 512, 1536], P('dp', 'seq')
All inputs are finite; a program needn't handle non-finite values.
Results may differ from a plain program's by a relative error of at most 0.0091.
Values may be sent and summed in bfloat16 or wider, within the bound.
A program may use at most 128 MiB of HBM per device.

v0:
```python
import math

import jax
import jax.numpy as jnp
from jax import lax
from jax.sharding import PartitionSpec as P


def padded_2(cells, sides, width):
    for axis, dim in sides:
        count = lax.axis_size(axis)
        ends = count - 1
        head = lax.slice_in_dim(cells, 0, width, axis=dim)
        tail = lax.slice_in_dim(cells, cells.shape[dim] - width, cells.shape[dim], axis=dim)
        cells = jnp.concatenate(
            [
                lax.ppermute(tail, axis, [(i, (i + 1) % count) for i in range(ends)]),
                cells,
                lax.ppermute(head, axis, [((i + 1) % count, i) for i in range(ends)]),
            ],
            axis=dim,
        )
    return cells


def add_taps(padded, weights, sequence_length):
    totals = jnp.zeros(padded.shape[:-2] + (sequence_length, weights.shape[2]), jnp.float32)
    for offset in range(weights.shape[0]):
        window_rows = lax.slice_in_dim(
            padded, offset, offset + sequence_length, axis=padded.ndim - 2
        )
        totals = totals + jnp.einsum(
            "...pc,cn->...pn", window_rows, weights[offset], preferred_element_type=jnp.float32
        )
    return totals


def make_block(queries, bias_fragments, score_scale):

    def attend_block(carry, piece, start):
        running_max, denominator, accumulated = carry
        key_rows, value_rows, key_codes = piece
        repeated_base_codes = jnp.concatenate((key_codes, key_codes, key_codes), axis=1)
        scores = (
            jnp.einsum("ihd,jd->hij", queries, key_rows, preferred_element_type=jnp.float32)
            * score_scale
        )
        scores = scores + jnp.einsum(
            "mrz,sz->mrs", bias_fragments, repeated_base_codes, preferred_element_type=jnp.float32
        )
        new_max = jnp.maximum(running_max, jnp.max(scores, axis=2))
        weights = jnp.exp(scores - new_max[:, :, None])
        multiplier = jnp.exp(running_max - new_max)
        denominator = denominator * multiplier + jnp.sum(weights, axis=2)
        accumulated = accumulated * multiplier[:, :, None] + jnp.einsum(
            "hij,jd->hid",
            weights.astype(jnp.bfloat16),
            value_rows,
            preferred_element_type=jnp.float32,
        )
        return (new_max, denominator, accumulated)

    return attend_block


def shards(
    signal,
    bases,
    base_table,
    conv_weight,
    batch_norm_gain,
    norm_bias,
    proj_weight,
    attn_gain,
    q_weight,
    k_weight,
    v_weight,
    bias_table,
    buckets,
    out_weight,
):
    signal_rows = signal[0]
    sequence_length = signal_rows.shape[0]
    channels = signal_rows.shape[1]
    base_onehot = (bases[0][:, None] == jnp.arange(4, dtype=jnp.int32)[None, :]).astype(
        jnp.bfloat16
    )
    embedded = (
        signal_rows.astype(jnp.float32)
        + jnp.dot(base_onehot, base_table, preferred_element_type=jnp.float32)
    ).astype(jnp.bfloat16)
    padded = padded_2(embedded, (("seq", 0),), 2)
    convolved = add_taps(
        padded, lax.all_gather(conv_weight, "dp", axis=2, tiled=True), sequence_length
    )
    number = sequence_length * lax.axis_size("seq") * lax.axis_size("dp")
    totals = lax.psum(jnp.sum(convolved, axis=0), ("dp", "seq"))
    average = totals / number
    centred = convolved - average
    variance = lax.psum(jnp.sum(centred * centred, axis=0), ("dp", "seq")) / number
    normed = jax.nn.gelu(centred * lax.rsqrt(variance + 1e-05) * batch_norm_gain + norm_bias)
    token_count = sequence_length // 4
    pooled_features = jnp.max(normed.reshape(token_count, 4, channels), axis=1).astype(jnp.bfloat16)
    tokens = jnp.dot(pooled_features, proj_weight, preferred_element_type=jnp.float32).astype(
        jnp.bfloat16
    )
    token_float = tokens.astype(jnp.float32)
    normalized = (
        token_float
        * lax.rsqrt(jnp.mean(token_float * token_float, axis=1, keepdims=True) + 1e-06)
        * attn_gain
    ).astype(jnp.bfloat16)
    head_size = k_weight.shape[1]
    head_count = q_weight.shape[1] // head_size
    bucket_count = bias_table.shape[1]
    queries = (
        jnp.dot(normalized, q_weight, preferred_element_type=jnp.float32)
        .astype(jnp.bfloat16)
        .reshape(token_count, head_count, head_size)
    )
    key_rows = jnp.dot(normalized, k_weight, preferred_element_type=jnp.float32).astype(
        jnp.bfloat16
    )
    value_rows = jnp.dot(normalized, v_weight, preferred_element_type=jnp.float32).astype(
        jnp.bfloat16
    )
    bucket_onehot = buckets[0][:, None] == jnp.arange(bucket_count, dtype=jnp.int32)[None, :]
    query_bias = jnp.einsum(
        "vt,wtk->wvk",
        bucket_onehot.astype(jnp.float32),
        bias_table,
        precision=lax.Precision.HIGHEST,
    )
    bias_high = query_bias.astype(jnp.bfloat16)
    remainder = query_bias - bias_high.astype(jnp.float32)
    bias_middle = remainder.astype(jnp.bfloat16)
    lower_bias_part = (remainder - bias_middle.astype(jnp.float32)).astype(jnp.bfloat16)
    bias_fragments = jnp.concatenate((bias_high, bias_middle, lower_bias_part), axis=2)
    key_codes = bucket_onehot.astype(jnp.bfloat16)
    attend_block = make_block(queries, bias_fragments, head_size ** (-0.5))
    initial = (
        jnp.full((head_count, token_count), -1e30, jnp.float32),
        jnp.zeros((head_count, token_count), jnp.float32),
        jnp.zeros((head_count, token_count, head_size), jnp.float32),
    )
    all_rows, all_values, all_codes = (
        lax.all_gather(key_rows, "seq", axis=0, tiled=True),
        lax.all_gather(value_rows, "seq", axis=0, tiled=True),
        lax.all_gather(key_codes, "seq", axis=0, tiled=True),
    )
    key_total = all_rows.shape[0]
    block_rows = math.gcd(512, key_total)
    block_count = key_total // block_rows
    stacked = (
        all_rows.reshape(block_count, block_rows, head_size),
        all_values.reshape(block_count, block_rows, head_size),
        all_codes.reshape(block_count, block_rows, bucket_count),
    )

    def scan_step(carry, piece):
        return (attend_block(carry, piece, 0), None)

    final_state, unused = lax.scan(scan_step, initial, stacked)
    running_max, denominator, accumulated = final_state
    attended = (
        jnp.transpose(accumulated / denominator[:, :, None], (1, 0, 2))
        .reshape(token_count, head_count * head_size)
        .astype(jnp.bfloat16)
    )
    mixed = jnp.dot(attended, out_weight, preferred_element_type=jnp.float32).astype(jnp.bfloat16)
    return (tokens[None], mixed[None])


def solution(mesh):
    placed = (
        P("dp", "seq", None),
        P("dp", "seq"),
        P(),
        P(None, None, "dp"),
        P(),
        P(),
        P(),
        P(),
        P(),
        P(),
        P(),
        P(),
        P("dp", "seq"),
        P(),
    )
    return jax.shard_map(
        shards,
        mesh=mesh,
        in_specs=placed,
        out_specs=(P("dp", "seq", None), P("dp", "seq", None)),
        check_vma=False,
    )
```

profile of v0, /device:TPU:0, one launch (start us, length us, event | category | flops | bytes accessed | tf_op | source)
XLA Modules:
  0.0 275.5 jit_solution(13016959128324744105)
XLA Ops:
  7.2 0.0 copy-start
  7.2 0.0 all-gather.2.cloned.1.call-start
  7.2 0.7 all-gather.2.cloned.1.call-update
  7.9 2.1 fusion.9
  10.0 0.0 copy-start.1
  10.1 1.1 copy-done.1
  11.2 1.3 collective-permute-start.1
  12.5 5.6 %collective-permute-start = (bf16[2,1408]{1,0:T(2,128)(2,1)S(1)}, bf16[2,1408]{1,0:T(2,128)(2,1)S(1)}, u32[]{:S(2)}, u32[]{:S(2)}) collective-permute-start(bf16[2,1408]{1,0:T(2,128)(2,1)S(1)} %get-tuple-element.20), channel_id=1, source_target_pairs={{0,1},{1,2},{2,3},{4,5},{5,6},{6,7},{8,9},{9,10},{10,11},{12,13},{... | collective-permute-start | bytes 16904 | tf_op jit(solution)/shard_map/ppermute | solution.py:17
  18.1 0.1 copy.17
  18.2 0.0 copy-done.12
  18.2 12.5 %all_gather.14 = bf16[512,32]{0,1:T(8,128)(2,1)S(1)} all-gather(bf16[128,32]{0,1:T(8,128)(2,1)S(1)} %fusion.52), channel_id=1, replica_groups=mesh['dp'=8,'seq'=4] {'seq'}, dimensions={0}, use_global_device_ids=true | all-gather | bytes 40960 | tf_op jit(solution)/shard_map/all_gather | solution.py:149
  30.7 0.2 fusion.53
  30.9 0.6 bitcast_convert_fusion
  31.6 0.7 fusion.51
  32.2 83.2 %all-gather.2.cloned.1.call-done = bf16[5,1408,1408]{1,2,0:T(8,128)(2,1)} async-done(((bf16[5,1408,176]{1,2,0:T(8,128)(2,1)}), bf16[5,1408,1408]{1,2,0:T(8,128)(2,1)}) %all-gather.2.cloned.1.call-update) | async-done | bytes 19824656 | tf_op jit(solution)/shard_map/all_gather | solution.py:94
  115.4 5.2 %fusion.2 = f32[512,1408]{1,0:T(8,128)S(1)} fusion(bf16[512,1408]{1,0:T(8,128)(2,1)} %copy-done.1, bf16[5,1408,1408]{1,2,0:T(8,128)(2,1)} %all-gather.2.cloned.1.call-done), kind=kOutput, calls=%fused_computation.6 | convolution fusion | flops 2030043136 | bytes 8290304 | tf_op jit(solution)/shard_map/...pc,cn->...pn/dot_general | solution.py:32
  120.7 0.0 collective-permute-done.1
  120.7 0.0 copy-done.2
  120.7 4.7 %fusion.1 = f32[512,1408]{1,0:T(8,128)S(1)} fusion(bf16[5,1408,1408]{1,2,0:T(8,128)(2,1)} %all-gather.2.cloned.1.call-done, bf16[512,1408]{1,0:T(8,128)(2,1)S(1)} %copy-done.2, bf16[2,1408]{1,0:T(2,128)(2,1)S(1)} %collective-permute-done.1), kind=kOutput, calls=%fused_computation.4 | convolution fusion | flops 2032926720 | bytes 8295936 | tf_op jit(solution)/shard_map/...pc,cn->...pn/dot_general | solution.py:32
  125.4 4.7 %fusion = f32[512,1408]{1,0:T(8,128)S(1)} fusion(bf16[5,1408,1408]{1,2,0:T(8,128)(2,1)} %all-gather.2.cloned.1.call-done, bf16[2,1408]{1,0:T(2,128)(2,1)S(1)} %collective-permute-done.1, bf16[512,1408]{1,0:T(8,128)(2,1)S(1)} %copy-done.2), kind=kOutput, calls=%fused_computation.2 | convolution fusion | flops 2032926720 | bytes 8295936 | tf_op jit(solution)/shard_map/...pc,cn->...pn/dot_general | solution.py:32
  130.1 0.0 collective-permute-done
  130.1 4.7 %fusion.3 = f32[512,1408]{1,0:T(8,128)S(1)} fusion(bf16[5,1408,1408]{1,2,0:T(8,128)(2,1)} %all-gather.2.cloned.1.call-done, bf16[512,1408]{1,0:T(8,128)(2,1)S(1)} %copy-done.2, bf16[2,1408]{1,0:T(2,128)(2,1)S(1)} %collective-permute-done), kind=kOutput, calls=%fused_computation.8 | convolution fusion | flops 2032926720 | bytes 8295936 | tf_op jit(solution)/shard_map/...pc,cn->...pn/dot_general | solution.py:32
  134.9 6.4 %fusion.64 = (f32[1408]{0:T(1024)S(1)}, f32[512,1408]{1,0:T(8,128)}) fusion(f32[512,1408]{1,0:T(8,128)S(1)} %fusion, f32[512,1408]{1,0:T(8,128)S(1)} %fusion.1, f32[512,1408]{1,0:T(8,128)S(1)} %fusion.2, f32[512,1408]{1,0:T(8,128)S(1)} %fusion.3, bf16[5,1408,1408]{1,2,0:T(8,128)(2,1)} %all-gather.2.cloned.1.call-done, ...), kind=kOutput, calls=%fused_computation.93 | convolution fusion | flops 2036529792 | bytes 19835904 | tf_op jit(solution)/shard_map/...pc,cn->...pn/dot_general | solution.py:32
  141.3 39.3 %psum.14 = f32[1408]{0:T(1024)S(1)} all-reduce(f32[1408]{0:T(1024)S(1)} %get-tuple-element.26), channel_id=1, replica_groups=mesh['dp'=8,'seq'=4] {'dp','seq'}, use_global_device_ids=true, to_apply=%region_1.0 | all-reduce | flops 1408 | bytes 11264 | tf_op jit(solution)/shard_map/psum | solution.py:97
  180.6 2.1 multiply_reduce_fusion
  182.7 41.3 %psum.15 = f32[1408]{0:T(1024)S(1)} all-reduce(f32[1408]{0:T(1024)S(1)} %multiply_reduce_fusion), channel_id=1, replica_groups=mesh['dp'=8,'seq'=4] {'dp','seq'}, use_global_device_ids=true, to_apply=%region_3.0 | all-reduce | flops 1408 | bytes 11264 | tf_op jit(solution)/shard_map/psum | solution.py:100
  224.0 4.2 %fusion.16 = bf16[512,1408]{1,0:T(8,128)(2,1)} fusion(f32[512,1408]{1,0:T(8,128)} %get-tuple-element.36, f32[1408]{0:T(1024)S(1)} %copy-done.9, f32[1408]{0:T(1024)S(1)} %copy-done.10, f32[1408]{0:T(1024)S(1)} %add_rsqrt_fusion, f32[1408]{0:T(1024)S(1)} %broadcast_multiply_fusion), kind=kLoop, calls=%fused_computation.23 | loop fusion | flops 9371648 | bytes 4347904 | tf_op jit(solution)/shard_map/mul | solution.py:101
  228.3 3.7 %reshape.51 = bf16[128,4,1408]{2,1,0:T(4,128)(2,1)} reshape(bf16[512,1408]{1,0:T(8,128)(2,1)} %fusion.16) | data formatting | bytes 2883584 | tf_op jit(solution)/shard_map/reshape | solution.py:103
  231.9 3.1 %reduce_max.19 = bf16[128,1408]{1,0:T(8,128)(2,1)S(1)} reduce(bf16[128,4,1408]{2,1,0:T(4,128)(2,1)} %reshape.51, bf16[]{:T(256)} %constant.131), dimensions={1}, to_apply=%region_4.0 | reduce | flops 540672 | bytes 1802242 | tf_op jit(solution)/shard_map/reduce_max | solution.py:103
  235.0 0.0 copy-start.11
  235.1 0.0 copy-start.13
  235.1 0.0 copy-start.14
  235.1 0.0 copy-start.3
  235.1 3.2 %fusion.32 = (f32[128]{0:T(128)S(1)}, bf16[128,1536]{1,0:T(8,128)(2,1)S(1)}) fusion(bf16[128,1408]{1,0:T(8,128)(2,1)S(1)} %reduce_max.19, bf16[1408,1536]{1,0:T(8,128)(2,1)} %param.20), kind=kOutput, calls=%fused_computation.53 | convolution fusion | flops 554434432 | bytes 5079552 | tf_op jit(solution)/shard_map/dot_general | solution.py:104
  238.3 0.0 copy-start.4
  238.4 0.0 copy-done.11
  238.4 0.0 copy-done.13
  238.4 0.4 convolution_convert_fusion.3
  238.7 12.4 %all_gather.15 = bf16[512,128]{0,1:T(8,128)(2,1)S(1)} all-gather(bf16[128,128]{0,1:T(8,128)(2,1)S(1)} %convolution_convert_fusion.3), channel_id=1, replica_groups=mesh['dp'=8,'seq'=4] {'seq'}, dimensions={0}, use_global_device_ids=true | all-gather | bytes 163840 | tf_op jit(solution)/shard_map/all_gather | solution.py:148
  251.2 0.3 convolution_convert_fusion.4
  251.5 13.3 %all_gather.13 = bf16[512,128]{1,0:T(8,128)(2,1)S(1)} all-gather(bf16[128,128]{1,0:T(8,128)(2,1)S(1)} %convolution_convert_fusion.4), channel_id=1, replica_groups=mesh['dp'=8,'seq'=4] {'seq'}, dimensions={0}, use_global_device_ids=true | all-gather | bytes 163840 | tf_op jit(solution)/shard_map/all_gather | solution.py:147
  264.9 0.6 fusion.29
  265.5 0.0 copy-done.4
  265.5 0.4 fusion.36
  266.0 0.5 fusion.65
  266.5 0.3 fusion.18
  266.8 0.5 fusion.28
  267.3 1.4 fusion.17
  (24 shorter events, 0.1 us)
Async XLA Ops:
  7.2 260.2 %copy-start = (bf16[1024,1536]{1,0:T(8,128)(2,1)S(1)}, bf16[1024,1536]{1,0:T(8,128)(2,1)}, u32[]{:S(2)}) copy-start(bf16[1024,1536]{1,0:T(8,128)(2,1)} %param.27) | copy-start | bytes 9437188
  7.2 10.9 %copy-start.8 = (f32[8,32,32]{2,1,0:T(8,128)S(1)}, f32[8,32,32]{2,1,0:T(8,128)}, u32[]{:S(2)}) copy-start(f32[8,32,32]{2,1,0:T(8,128)} %param.25) | copy-start | bytes 98308
  7.2 11.0 %copy-start.12 = (s32[1,128]{1,0:T(1,128)S(1)}, s32[1,128]{1,0:T(1,128)}, u32[]{:S(2)}) copy-start(s32[1,128]{1,0:T(1,128)} %param.26) | copy-start | bytes 1540
  7.2 108.2 %all-gather.2.cloned.1.call-start = ((), (), s32[]{:S(2)}) async-start(), calls=%async_computation | async-start | bytes 22302720 | tf_op jit(solution)/shard_map/all_gather | solution.py:94
  10.0 1.1 copy-start.1
  11.2 109.5 %collective-permute-start.1 = (bf16[2,1408]{1,0:T(2,128)(2,1)S(1)}, bf16[2,1408]{1,0:T(2,128)(2,1)S(1)}, u32[]{:S(2)}, u32[]{:S(2)}) collective-permute-start(bf16[2,1408]{1,0:T(2,128)(2,1)S(1)} %get-tuple-element.21), channel_id=1, source_target_pairs={{1,0},{2,1},{3,2},{5,4},{6,5},{7,6},{9,8},{10,9},{11,10},{13,12},{... | collective-permute-start | bytes 16904 | tf_op jit(solution)/shard_map/ppermute | solution.py:19
  12.5 117.7 %collective-permute-start = (bf16[2,1408]{1,0:T(2,128)(2,1)S(1)}, bf16[2,1408]{1,0:T(2,128)(2,1)S(1)}, u32[]{:S(2)}, u32[]{:S(2)}) collective-permute-start(bf16[2,1408]{1,0:T(2,128)(2,1)S(1)} %get-tuple-element.20), channel_id=1, source_target_pairs={{0,1},{1,2},{2,3},{4,5},{5,6},{6,7},{8,9},{9,10},{10,11},{12,13},{... | collective-permute-start | bytes 16904 | tf_op jit(solution)/shard_map/ppermute | solution.py:17
  115.4 5.3 %copy-start.2 = (bf16[512,1408]{1,0:T(8,128)(2,1)S(1)}, bf16[512,1408]{1,0:T(8,128)(2,1)}, u32[]{:S(2)}) copy-start(bf16[512,1408]{1,0:T(8,128)(2,1)} %copy-done.1) | copy-start | bytes 4325380
  141.3 82.8 %copy-start.9 = (f32[1408]{0:T(1024)S(1)}, f32[1408]{0:T(1024)}, u32[]{:S(2)}) copy-start(f32[1408]{0:T(1024)} %param.19) | copy-start | bytes 16900
  141.3 82.8 %copy-start.10 = (f32[1408]{0:T(1024)S(1)}, f32[1408]{0:T(1024)}, u32[]{:S(2)}) copy-start(f32[1408]{0:T(1024)} %param.18) | copy-start | bytes 16900
  235.0 3.3 %copy-start.11 = (f32[1536]{0:T(1024)S(1)}, f32[1536]{0:T(1024)}, u32[]{:S(2)}) copy-start(f32[1536]{0:T(1024)} %param.21) | copy-start | bytes 18436
  235.1 3.3 %copy-start.13 = (bf16[1536,128]{1,0:T(8,128)(2,1)S(1)}, bf16[1536,128]{1,0:T(8,128)(2,1)}, u32[]{:S(2)}) copy-start(bf16[1536,128]{1,0:T(8,128)(2,1)} %param.24) | copy-start | bytes 1179652
  235.1 16.1 %copy-start.14 = (bf16[1536,128]{1,0:T(8,128)(2,1)S(1)}, bf16[1536,128]{1,0:T(8,128)(2,1)}, u32[]{:S(2)}) copy-start(bf16[1536,128]{1,0:T(8,128)(2,1)} %param.23) | copy-start | bytes 1179652
  235.1 29.8 %copy-start.3 = (bf16[1536,1024]{1,0:T(8,128)(2,1)S(1)}, bf16[1536,1024]{1,0:T(8,128)(2,1)}, u32[]{:S(2)}) copy-start(bf16[1536,1024]{1,0:T(8,128)(2,1)} %param.22) | copy-start | bytes 9437188
  238.3 27.2 %copy-start.4 = (bf16[128,1536]{1,0:T(8,128)(2,1)}, bf16[128,1536]{1,0:T(8,128)(2,1)S(1)}, u32[]{:S(2)}) copy-start(bf16[128,1536]{1,0:T(8,128)(2,1)S(1)} %get-tuple-element.38) | copy-start | bytes 1179652
  264.8 1.1 copy-start.5
  264.8 1.1 copy-start.6
  264.9 1.1 copy-start.7
Sparse Core Ops, SparseCore 0:
  9.9 105.4 all-gather.1
where the time goes:
time: 276 us
  blocking collectives  119 us (43%)
  waiting for transfers between devices  83.9 us (30%)
  matrix products  35.4 us (13%)
  between operations  14.4 us (5%)
  other arithmetic  11.1 us (4%)
  starting transfers between devices  6.89 us (2%)
  local copies, waits for them, and re-layouts  4.95 us (2%)
    all_gather x1, waiting for transfers between devices, shards(): lax.all_gather(conv_weight, 'dp', axis=2, tiled=True)  83.2 us
    psum x1, blocking collectives, shards(): lax.psum(jnp.sum(centred * centred, axis=0), ('dp', 'seq')) / number  41.3 us
    psum x1, blocking collectives, shards(): totals = lax.psum(jnp.sum(convolved, axis=0), ('dp', 'seq'))  39.3 us
    dot_general x5, matrix products, add_taps(): jnp.einsum('...pc,cn->...pn', window_rows, weights[offset], preferred_ele...  25.8 us
    all_gather x1, blocking collectives, shards(): lax.all_gather(key_rows, 'seq', axis=0, tiled=True)  13.3 us
    all_gather x1, blocking collectives, shards(): lax.all_gather(key_codes, 'seq', axis=0, tiled=True)  12.5 us
    all_gather x1, blocking collectives, shards(): lax.all_gather(value_rows, 'seq', axis=0, tiled=True)  12.4 us
    ppermute x1, starting transfers between devices, padded_2(): lax.ppermute(tail, axis, [(i, (i + 1) % count) for i in range(ends)])  5.56 us
  transfers between devices with their start and end apart: 3, of which 1 were waited for; matrix products, arithmetic and copies ran while one was open for 7% of the time, Pallas kernels for 0%

commit v1 on v0

--- a/solution.py
+++ b/solution.py
@@ -1,8 +1,11 @@
+import functools
 import math
 
 import jax
 import jax.numpy as jnp
 from jax import lax
+from jax.experimental import pallas as pl
+from jax.experimental.pallas import tpu as pltpu
 from jax.sharding import PartitionSpec as P
 
 
@@ -171,6 +174,542 @@
     return (tokens[None], mixed[None])
 
 
+PLANES = 4
+MESH_IDS = pl.DeviceIdType.MESH
+
+
+def block_kernel(
+    cuts,
+    planes_ref,
+    taps_ref,
+    gain_ref,
+    shift_ref,
+    proj_ref,
+    attn_gain_ref,
+    q_ref,
+    k_ref,
+    v_ref,
+    table_ref,
+    key_codes_ref,
+    query_codes_ref,
+    out_ref,
+    tokens_ref,
+    mixed_ref,
+    cells,
+    taps,
+    sums,
+    halo,
+    edges,
+    codes,
+    stats,
+    staged,
+    pooled,
+    kv,
+    bias,
+    proj,
+    q_w,
+    kv_w,
+    out_w,
+    attended,
+    load_sem,
+    halo_send,
+    halo_recv,
+    edge_send,
+    edge_recv,
+    code_send,
+    code_recv,
+    core_send,
+    core_recv,
+    x_send,
+    x_recv,
+    pass_send,
+    pass_recv,
+    tap_send,
+    tap_recv,
+    tap_pass_send,
+    tap_pass_recv,
+    stat_send,
+    stat_recv,
+    pool_send,
+    pool_recv,
+    kv_send,
+    kv_recv,
+):
+    place = lax.axis_index("dp")
+    z = lax.axis_index("seq")
+    depth = lax.axis_size("seq")
+    core, x, y = place % 2, (place // 2) % 2, place // 4
+
+    def at(y_of, x_of, core_of):
+        return (y_of * 2 + x_of) * 2 + core_of
+
+    slots = (
+        place,
+        at(y, x, 1 - core),
+        at(y, 1 - x, core),
+        at(y, 1 - x, 1 - core),
+    )
+    across = at(1 - y, x, core)
+    columns = (place, across)
+    ring = [(z + step) % depth for step in range(depth)]
+    mate = z + 1 - 2 * (z % 2)
+    rank = y * depth + z
+
+    def copy(source, target, send, receive, device):
+        return pltpu.make_async_remote_copy(
+            src_ref=source,
+            dst_ref=target,
+            send_sem=send,
+            recv_sem=receive,
+            device_id=device,
+            device_id_type=MESH_IDS,
+        )
+
+    loads = [
+        pltpu.make_async_copy(planes_ref, cells.at[0, 2:6], load_sem.at[0]),
+        pltpu.make_async_copy(taps_ref, taps.at[0], load_sem.at[1]),
+        pltpu.make_async_copy(proj_ref, proj, load_sem.at[2]),
+        pltpu.make_async_copy(q_ref, q_w, load_sem.at[3]),
+        pltpu.make_async_copy(k_ref, kv_w.at[:, 0:128], load_sem.at[4]),
+        pltpu.make_async_copy(v_ref, kv_w.at[:, 128:256], load_sem.at[5]),
+        pltpu.make_async_copy(out_ref, out_w, load_sem.at[6]),
+    ]
+    for load in loads:
+        load.start()
+
+    codes[z] = key_codes_ref[...]
+    halo[...] = jnp.zeros_like(halo)
+
+    barrier = pltpu.get_barrier_semaphore()
+    partners = [(slots[s], z) for s in (1, 2, 3)] + [(across, z)]
+    for step in range(1, depth):
+        partners += [(place, ring[step]), (across, ring[step])]
+    for partner in partners:
+        pl.semaphore_signal(barrier, inc=1, device_id=partner, device_id_type=MESH_IDS)
+    loads[0].wait()
+    pl.semaphore_wait(barrier, len(partners))
+
+    rows = cells.shape[2]
+    to_left = copy(
+        cells.at[0, 2:4, 0:16], halo.at[1], halo_send.at[0], halo_recv.at[1], (place, z - 1)
+    )
+    to_right = copy(
+        cells.at[0, 4:6, rows - 16 : rows],
+        halo.at[0],
+        halo_send.at[1],
+        halo_recv.at[0],
+        (place, z + 1),
+    )
+    pl.when(z > 0)(to_left.start)
+    pl.when(z < depth - 1)(to_right.start)
+
+    half = (taps.shape[2] // 16 + 1) // 2 * 16
+    halves = (slice(0, half), slice(half, taps.shape[2]))
+
+    def by_parity(act):
+        for parity in (0, 1):
+            pl.when(z % 2 == parity)(functools.partial(act, halves[parity], halves[1 - parity]))
+
+    def own_to_x(i):
+        part = cells.at[0, 2:6, :, cuts[i]]
+        return copy(
+            part, cells.at[2, 2:6, :, cuts[i]], x_send.at[i], x_recv.at[i], (slots[2], z)
+        )
+
+    def own_to_core(i):
+        part = cells.at[0, 2:6, :, cuts[i]]
+        return copy(
+            part, cells.at[1, 2:6, :, cuts[i]], core_send.at[i], core_recv.at[i], (slots[1], z)
+        )
+
+    def pass_on(i):
+        part = cells.at[2, 2:6, :, cuts[i]]
+        return copy(
+            part, cells.at[3, 2:6, :, cuts[i]], pass_send.at[i], pass_recv.at[i], (slots[1], z)
+        )
+
+    def taps_across(i, mine):
+        return copy(
+            taps.at[0, :, mine, cuts[i]],
+            taps.at[1, :, mine, cuts[i]],
+            tap_send.at[i],
+            tap_recv.at[i],
+            (across, z),
+        )
+
+    def taps_pass(i, part):
+        return copy(
+            taps.at[1, :, part, cuts[i]],
+            taps.at[1, :, part, cuts[i]],
+            tap_pass_send.at[i],
+            tap_pass_recv.at[i],
+            (place, mate),
+        )
+
+    number = len(cuts)
+    for i in range(number):
+        own_to_x(i).start()
+        if i == 0:
+            loads[1].wait()
+        by_parity(lambda mine, other: taps_across(i, mine).start())
+        own_to_core(i).start()
+
+    code_copies = [
+        copy(codes.at[z], codes.at[z], code_send.at[s], code_recv.at[s], (place, ring[s]))
+        for s in range(1, depth)
+    ]
+    for item in code_copies:
+        item.start()
+
+    pl.when(z > 0)(lambda: copy(
+        cells.at[0, 2:4, 0:16], halo.at[0], halo_send.at[0], halo_recv.at[0], (place, z - 1)
+    ).wait_recv())
+    pl.when(z < depth - 1)(lambda: copy(
+        cells.at[0, 2:4, 0:16], halo.at[1], halo_send.at[0], halo_recv.at[1], (place, z + 1)
+    ).wait_recv())
+    row = lax.broadcasted_iota(jnp.int32, (16, 1), 0)
+    before = halo[0].astype(jnp.float32)
+    after = halo[1].astype(jnp.float32)
+    edge = jnp.where(row == 0, before[0, 15:16], 0.0)
+    edge = jnp.where(row == 1, before[1, 15:16], edge)
+    edge = jnp.where(row == 2, after[0, 0:1], edge)
+    edge = jnp.where(row == 3, after[1, 0:1], edge)
+    edges[0] = edge.astype(jnp.bfloat16)
+    edge_copies = [
+        copy(edges.at[0], edges.at[s], edge_send.at[s], edge_recv.at[s], (slots[s], z))
+        for s in (1, 2, 3)
+    ]
+    for item in edge_copies:
+        item.start()
+
+    for item in code_copies:
+        item.wait_recv()
+    heads = table_ref.shape[0]
+
+    def add_bias(head, carry):
+        table = table_ref[head]
+        rest = table
+        for part in range(3):
+            piece = rest.astype(jnp.bfloat16)
+            rest = rest - piece.astype(jnp.float32)
+            of_query = jnp.dot(
+                query_codes_ref[...], piece, preferred_element_type=jnp.float32
+            ).astype(jnp.bfloat16)
+            for s in range(depth):
+                block = jnp.dot(of_query, codes[s], preferred_element_type=jnp.float32)
+                columns_of = slice(s * 128, (s + 1) * 128)
+                if part == 0:
+                    bias[head, :, columns_of] = block
+                else:
+                    bias[head, :, columns_of] += block
+        return carry
+
+    lax.fori_loop(0, heads, add_bias, 0)
+    for item in edge_copies:
+        item.wait_recv()
+
+    def convolve(i):
+        cut = cuts[i]
+
+        def one_window(slot, carry):
+            fringe = edges[slot, :, cut].astype(jnp.float32)
+            line = lax.broadcasted_iota(jnp.int32, (rows, 1), 0)
+            for target, source, edge_row in ((0, 4, 0), (1, 5, 1), (6, 2, 2), (7, 3, 3)):
+                values = cells[slot, source, :, cut].astype(jnp.float32)
+                if target < 2:
+                    moved, end = pltpu.roll(values, 1, 0), 0
+                else:
+                    moved, end = pltpu.roll(values, rows - 1, 0), rows - 1
+                cells[slot, target, :, cut] = jnp.where(
+                    line == end, fringe[edge_row : edge_row + 1], moved
+                ).astype(jnp.bfloat16)
+            for side in range(2):
+                total = None
+                for t in range(taps.shape[1]):
+                    part = cells[slot, t : t + PLANES, :, cut].reshape(PLANES * rows, -1)
+                    term = lax.dot_general(
+                        part,
+                        taps[side, t, :, cut],
+                        (((1,), (1,)), ((), ())),
+                        preferred_element_type=jnp.float32,
+                    )
+                    total = term if total is None else total + term
+                if i == 0:
+                    sums[slot, side] = total
+                else:
+                    sums[slot, side] += total
+            return carry
+
+        lax.fori_loop(0, 4, one_window, 0)
+
+    def arrive(i):
+        own_to_core(i).wait_recv()
+        pass_on(i).wait_recv()
+        by_parity(lambda mine, other: taps_pass(i, other).wait_recv())
+
+    for i in range(number):
+        own_to_x(i).wait_recv()
+        pass_on(i).start()
+        by_parity(lambda mine, other: taps_across(i, mine).wait_recv())
+        by_parity(lambda mine, other: taps_pass(i, mine).start())
+        if i:
+            arrive(i - 1)
+            convolve(i - 1)
+    arrive(number - 1)
+    convolve(number - 1)
+
+    local = 4 * PLANES * rows
+    line = lax.broadcasted_iota(jnp.int32, (8, 1), 0)
+    for side, owner_y in ((0, y), (1, 1 - y)):
+        mean = sum(jnp.sum(sums[s, side], axis=0, keepdims=True) for s in range(4)) / local
+        squares = sum(
+            jnp.sum(jnp.square(sums[s, side] - mean), axis=0, keepdims=True) for s in range(4)
+        )
+        stats[rank, owner_y] = jnp.where(line == 0, mean, jnp.where(line == 1, squares, 0.0))
+    stat_copies = []
+    for dy, y_to in ((0, y), (1, 1 - y)):
+        for step in range(depth):
+            if dy or step:
+                n = dy * depth + step
+                stat_copies.append(
+                    copy(
+                        stats.at[rank],
+                        stats.at[rank],
+                        stat_send.at[n],
+                        stat_recv.at[n],
+                        (at(y_to, x, core), ring[step]),
+                    )
+                )
+    for item in stat_copies:
+        item.start()
+    for item in stat_copies:
+        item.wait_recv()
+    ranks = 2 * depth
+
+    def normalise(side, owner_y, column):
+        means = [stats[r, owner_y, 0:1] for r in range(ranks)]
+        mean = sum(means) / ranks
+        squares = sum(stats[r, owner_y, 1:2] for r in range(ranks))
+        squares = squares + local * sum(jnp.square(m - mean) for m in means)
+        factor = lax.rsqrt(squares / (local * ranks) + 1e-05) * gain_ref[column]
+        shift = shift_ref[column]
+
+        def activate(slot):
+            cube = sums[slot, side].reshape(PLANES, rows, -1)
+            cube = (cube - mean) * factor + shift
+            top, low = jnp.max(cube, axis=0), jnp.min(cube, axis=0)
+            return jnp.maximum(jax.nn.gelu(top), jax.nn.gelu(low)).astype(jnp.bfloat16)
+
+        return activate
+
+    activations = [normalise(0, y, columns[0]), normalise(1, 1 - y, columns[1])]
+    pool_copies = []
+    for slot in (3, 2, 1):
+        for side in (0, 1):
+            staged[slot, side] = activations[side](slot)
+            item = copy(
+                staged.at[slot, side],
+                pooled.at[columns[side]],
+                pool_send.at[slot, side],
+                pool_recv.at[slot, side],
+                (slots[slot], z),
+            )
+            item.start()
+            pool_copies.append(item)
+    for side in (0, 1):
+        pooled[columns[side]] = activations[side](0)
+    for load in loads[2:]:
+        load.wait()
+    for item in pool_copies:
+        item.wait_recv()
+
+    share = pooled.shape[2]
+    total = None
+    for d in range(pooled.shape[0]):
+        term = jnp.dot(
+            pooled[d], proj[d * share : (d + 1) * share], preferred_element_type=jnp.float32
+        )
+        total = term if total is None else total + term
+    tokens = total.astype(jnp.bfloat16)
+    tokens_ref[...] = tokens
+    wide = tokens.astype(jnp.float32)
+    normalized = (
+        wide
+        * lax.rsqrt(jnp.mean(wide * wide, axis=1, keepdims=True) + 1e-06)
+        * attn_gain_ref[...]
+    ).astype(jnp.bfloat16)
+    kv[z] = jnp.dot(normalized, kv_w[...], preferred_element_type=jnp.float32).astype(
+        jnp.bfloat16
+    )
+    kv_copies = [
+        copy(kv.at[z], kv.at[z], kv_send.at[s], kv_recv.at[s], (place, ring[s]))
+        for s in range(1, depth)
+    ]
+    for item in kv_copies:
+        item.start()
+    queries = jnp.dot(normalized, q_w[...], preferred_element_type=jnp.float32).astype(
+        jnp.bfloat16
+    )
+    for item in kv_copies:
+        item.wait_recv()
+    keys = kv[:, :, 0:128].reshape(depth * rows, 128)
+    values = kv[:, :, 128:256].reshape(depth * rows, 128)
+    for head in range(heads):
+        lanes = slice(head * 128, (head + 1) * 128)
+        scores = lax.dot_general(
+            queries[:, lanes],
+            keys,
+            (((1,), (1,)), ((), ())),
+            preferred_element_type=jnp.float32,
+        )
+        scores = scores * (128**-0.5) + bias[head]
+        weights = jnp.exp(scores - jnp.max(scores, axis=1, keepdims=True))
+        denominator = jnp.sum(weights, axis=1, keepdims=True)
+        summed = jnp.dot(weights.astype(jnp.bfloat16), values, preferred_element_type=jnp.float32)
+        attended[:, lanes] = (summed / denominator).astype(jnp.bfloat16)
+    mixed_ref[...] = jnp.dot(
+        attended[...], out_w[...], preferred_element_type=jnp.float32
+    ).astype(jnp.bfloat16)
+
+    pl.when(z > 0)(to_left.wait_send)
+    pl.when(z < depth - 1)(to_right.wait_send)
+    for i in range(number):
+        own_to_x(i).wait_send()
+        own_to_core(i).wait_send()
+        pass_on(i).wait_send()
+        by_parity(lambda mine, other: taps_across(i, mine).wait_send())
+        by_parity(lambda mine, other: taps_pass(i, mine).wait_send())
+    for item in code_copies + edge_copies + stat_copies + pool_copies + kv_copies:
+        item.wait_send()
+
+
+def fused_shards(
+    signal,
+    bases,
+    base_table,
+    conv_weight,
+    batch_norm_gain,
+    norm_bias,
+    proj_weight,
+    attn_gain,
+    q_weight,
+    k_weight,
+    v_weight,
+    bias_table,
+    buckets,
+    out_weight,
+):
+    positions, channels = signal.shape[1:]
+    rows = positions // PLANES
+    devices, depth = lax.axis_size("dp"), lax.axis_size("seq")
+    width = conv_weight.shape[0]
+    share = conv_weight.shape[2]
+    heads, classes = bias_table.shape[:2]
+    model = proj_weight.shape[1]
+    base_onehot = (bases[0][:, None] == jnp.arange(4, dtype=jnp.int32)[None, :]).astype(
+        jnp.bfloat16
+    )
+    embedded = (
+        signal[0].astype(jnp.float32)
+        + jnp.dot(base_onehot, base_table, preferred_element_type=jnp.float32)
+    ).astype(jnp.bfloat16)
+    planes = jnp.transpose(embedded.reshape(rows, PLANES, channels), (1, 0, 2))
+    taps = jnp.transpose(conv_weight, (0, 2, 1))
+    kinds = jnp.arange(classes, dtype=jnp.int32)
+    query_codes = (buckets[0][:, None] == kinds[None, :]).astype(jnp.bfloat16)
+    key_codes = (kinds[:, None] == buckets[0][None, :]).astype(jnp.bfloat16)
+    cuts = tuple(
+        slice(start, min(start + 256, channels)) for start in range(0, channels, 256)
+    )
+    number = len(cuts)
+    vmem = pl.BlockSpec(memory_space=pltpu.VMEM)
+    anywhere = pl.BlockSpec(memory_space=pl.ANY)
+    dma = pltpu.SemaphoreType.DMA
+    narrow, wide = jnp.bfloat16, jnp.float32
+    tokens, mixed = pl.pallas_call(
+        functools.partial(block_kernel, cuts),
+        out_shape=[jax.ShapeDtypeStruct((rows, model), narrow)] * 2,
+        in_specs=[
+            anywhere,
+            anywhere,
+            vmem,
+            vmem,
+            anywhere,
+            vmem,
+            anywhere,
+            anywhere,
+            anywhere,
+            vmem,
+            vmem,
+            vmem,
+            anywhere,
+        ],
+        out_specs=[vmem, vmem],
+        scratch_shapes=[
+            pltpu.VMEM((4, PLANES + width - 1, rows, channels), narrow),
+            pltpu.VMEM((2, width, share, channels), narrow),
+            pltpu.VMEM((4, 2, positions, share), wide),
+            pltpu.VMEM((2, 2, 16, channels), narrow),
+            pltpu.VMEM((4, 16, channels), narrow),
+            pltpu.VMEM((depth, classes, rows), narrow),
+            pltpu.VMEM((2 * depth, 2, 8, share), wide),
+            pltpu.VMEM((4, 2, rows, share), narrow),
+            pltpu.VMEM((devices, rows, share), narrow),
+            pltpu.VMEM((depth, rows, 256), narrow),
+            pltpu.VMEM((heads, rows, depth * rows), wide),
+            pltpu.VMEM(proj_weight.shape, narrow),
+            pltpu.VMEM(q_weight.shape, narrow),
+            pltpu.VMEM((model, 256), narrow),
+            pltpu.VMEM(out_weight.shape, narrow),
+            pltpu.VMEM((rows, q_weight.shape[1]), narrow),
+            dma((7,)),
+            dma((2,)),
+            dma((2,)),
+            dma((4,)),
+            dma((4,)),
+            dma((depth,)),
+            dma((depth,)),
+            dma((number,)),
+            dma((number,)),
+            dma((number,)),
+            dma((number,)),
+            dma((number,)),
+            dma((number,)),
+            dma((number,)),
+            dma((number,)),
+            dma((number,)),
+            dma((number,)),
+            dma((2 * depth,)),
+            dma((2 * depth,)),
+            dma((4, 2)),
+            dma((4, 2)),
+            dma((depth,)),
+            dma((depth,)),
+        ],
+        compiler_params=pltpu.CompilerParams(
+            collective_id=0, has_side_effects=True, vmem_limit_bytes=52 * 1024 * 1024
+        ),
+        cost_estimate=pl.CostEstimate(
+            flops=12_000_000_000, bytes_accessed=20_000_000, transcendentals=4_000_000
+        ),
+    )(
+        planes,
+        taps,
+        batch_norm_gain.reshape(devices, 1, share),
+        norm_bias.reshape(devices, 1, share),
+        proj_weight,
+        attn_gain[None],
+        q_weight,
+        k_weight,
+        v_weight,
+        bias_table,
+        key_codes,
+        query_codes,
+        out_weight,
+    )
+    return (tokens[None], mixed[None])
+
+
 def solution(mesh):
     placed = (
         P("dp", "seq", None),
@@ -188,8 +727,9 @@
         P("dp", "seq"),
         P(),
     )
+    whole_cube = mesh.shape["dp"] == 8 and mesh.shape["seq"] == 4
     return jax.shard_map(
-        shards,
+        fused_shards if whole_cube else shards,
         mesh=mesh,
         in_specs=placed,
         out_specs=(P("dp", "seq", None), P("dp", "seq", None)),

time: 276 us -> 108 us (0.39)
  blocking collectives: 119 us -> 0 us
  Pallas kernels: 0 us -> 97.3 us
  waiting for transfers between devices: 83.9 us -> 0 us
  matrix products: 35.4 us -> 3.08 us
  between operations: 14.4 us -> 0.76 us
  other arithmetic: 11.1 us -> 0.09 us
  starting transfers between devices: 6.89 us -> 0 us
    pallas_call x0 -> x1, Pallas kernels: none -> 97.3 us  [fused_shards(): pl.pallas_call(functools.partial(block_kernel, cuts), out_shape=[jax.Shap...]
    all_gather x1 -> x0, waiting for transfers between devices: 83.2 us -> none  [shards(): lax.all_gather(conv_weight, 'dp', axis=2, tiled=True)]
    psum x2 -> x0, blocking collectives: 80.6 us -> none  [the longest x1 41.3 us: shards(): lax.psum(jnp.sum(centred * centred, axis=0), ('dp', 'seq')) / number]
    all_gather x3 -> x0, blocking collectives: 38.3 us -> none  [the longest x1 13.3 us: shards(): lax.all_gather(key_rows, 'seq', axis=0, tiled=True)]
    dot_general x14 -> x1, matrix products: 35.2 us -> 3.08 us  [fused_shards(): jnp.dot(base_onehot, base_table, preferred_element_type=jnp.float32)]
    ppermute x2 -> x0, starting transfers between devices: 6.85 us -> none  [the longest x1 5.56 us: padded_2(): lax.ppermute(tail, axis, [(i, (i + 1) % count) for i in range(ends)])]
    mul x2 -> x0, other arithmetic: 4.23 us -> none  [the longest x1 4.23 us: shards(): jax.nn.gelu(centred * lax.rsqrt(variance + 1e-05) * batch_norm_gain + nor...]
    reduce_max x1 -> x0, other arithmetic: 3.12 us -> none  [shards(): jnp.max(normed.reshape(token_count, 4, channels), axis=1)]
  transfers between devices with their start and end apart: 3 -> 0, of which waited for: 1 -> 0; matrix products, arithmetic and copies ran while one was open for 7% -> 0% of each run, Pallas kernels for 0% -> 0%
where the time goes in v1:
time: 108 us
  Pallas kernels  97.3 us (90%)
  local copies, waits for them, and re-layouts  6.51 us (6%)
  matrix products  3.08 us (3%)
    pallas_call x1, Pallas kernels, fused_shards(): pl.pallas_call(functools.partial(block_kernel, cuts), out_shape=[jax.Shap...  97.3 us
    reshape x2, local copies, waits for them, and re-layouts, fused_shards(): planes = jnp.transpose(embedded.reshape(rows, PLANES, channels), (1, 0, 2))  4.09 us
    dot_general x1, matrix products, fused_shards(): jnp.dot(base_onehot, base_table, preferred_element_type=jnp.float32)  3.08 us
    unnamed x18, local copies, waits for them, and re-layouts  2.23 us

profile of v1, /device:TPU:0, one launch (start us, length us, event | category | flops | bytes accessed | tf_op | source)
XLA Modules:
  0.0 107.7 jit_solution(13219320997254879216)
XLA Ops:
  0.6 0.0 copy-start
  0.6 0.7 copy-done
  1.3 3.1 %fusion = bf16[512,1408]{1,0:T(8,128)(2,1)} fusion(bf16[4,1408]{1,0:T(4,128)(2,1)S(1)} %copy-done, bf16[1,512,1408]{2,1,0:T(8,128)(2,1)} %param.14, s32[512]{0:T(512)} %bitcast.17), kind=kOutput, calls=%fused_computation.1 | convolution fusion | flops 7931904 | bytes 2896896 | tf_op jit(solution)/shard_map/dot_general | solution.py:614
  4.4 0.0 copy-start.5
  4.4 0.0 copy-start.6
  4.4 0.0 copy-start.4
  4.4 0.0 copy-start.7
  4.4 0.0 copy-start.1
  4.4 0.0 copy-start.2
  4.5 0.0 copy-start.3
  4.5 2.8 %reshape.17 = bf16[128,4,1408]{2,1,0:T(4,128)(2,1)S(1)} reshape(bf16[512,1408]{1,0:T(8,128)(2,1)} %fusion) | data formatting | bytes 2883584 | tf_op jit(solution)/shard_map/reshape | solution.py:616
  7.3 1.3 %copy.18 = bf16[128,4,1408]{2,0,1:T(8,128)(2,1)} copy(bf16[128,4,1408]{2,1,0:T(4,128)(2,1)S(1)} %reshape.17) | data formatting | bytes 2883584 | tf_op jit(solution)/shard_map/reshape | solution.py:616
  8.6 0.0 copy-done.5
  8.6 0.1 reshape.18.gain_ref
  8.7 0.0 copy-done.6
  8.7 0.1 reshape.19.shift_ref
  8.8 0.0 copy-done.4
  8.8 0.0 copy-done.7
  8.8 0.1 fusion.2.query_codes_ref
  8.9 0.0 copy-done.1
  8.9 0.0 copy-done.2
  8.9 0.0 copy-done.3
  8.9 97.3 %shard_map.149 = (bf16[128,1536]{1,0:T(8,128)(2,1)S(1)}, bf16[128,1536]{1,0:T(8,128)(2,1)S(1)}) custom-call(bf16[4,128,1408]{2,1,0:T(8,128)(2,1)} %bitcast.14, bf16[5,176,1408]{2,1,0:T(8,128)(2,1)} %bitcast.18, f32[8,1,176]{2,1,0:T(1,128)S(1)} %reshape.18.gain_ref, f32[8,1,176]{2,1,0:T(1,128)S(1)} %reshape.19.shift_ref, bf16[1408,1536]{1,0:T(8,128)(2,1)} %proj_ref.1, ...), custom_call_target="tpu_custom_call" | custom-call | flops 12000000000 | bytes 20000000 | tf_op jit(solution)/shard_map/pallas_call | solution.py:629
  106.3 0.7 copy.21
  107.0 0.7 copy.22
  (2 shorter events, 0.0 us)
Async XLA Ops:
  0.6 0.7 copy-start
  4.4 4.2 %copy-start.5 = (f32[1408]{0:T(1024)S(1)}, f32[1408]{0:T(1024)}, u32[]{:S(2)}) copy-start(f32[1408]{0:T(1024)} %param.18) | copy-start | bytes 16900
  4.4 4.2 %copy-start.6 = (f32[1408]{0:T(1024)S(1)}, f32[1408]{0:T(1024)}, u32[]{:S(2)}) copy-start(f32[1408]{0:T(1024)} %param.19) | copy-start | bytes 16900
  4.4 4.3 %copy-start.4 = (f32[1536]{0:T(1024)S(1)}, f32[1536]{0:T(1024)}, u32[]{:S(2)}) copy-start(f32[1536]{0:T(1024)} %param.21) | copy-start | bytes 18436
  4.4 4.4 %copy-start.7 = (s32[1,128]{1,0:T(1,128)S(1)}, s32[1,128]{1,0:T(1,128)}, u32[]{:S(2)}) copy-start(s32[1,128]{1,0:T(1,128)} %param.26) | copy-start | bytes 1540
  4.4 4.5 %copy-start.1 = (bf16[1536,128]{1,0:T(8,128)(2,1)S(1)}, bf16[1536,128]{1,0:T(8,128)(2,1)}, u32[]{:S(2)}) copy-start(bf16[1536,128]{1,0:T(8,128)(2,1)} %k_ref.1) | copy-start | bytes 1179652
  4.4 4.5 %copy-start.2 = (bf16[1536,128]{1,0:T(8,128)(2,1)S(1)}, bf16[1536,128]{1,0:T(8,128)(2,1)}, u32[]{:S(2)}) copy-start(bf16[1536,128]{1,0:T(8,128)(2,1)} %v_ref.1) | copy-start | bytes 1179652
  4.5 4.5 %copy-start.3 = (f32[8,32,32]{2,1,0:T(8,128)S(1)}, f32[8,32,32]{2,1,0:T(8,128)}, u32[]{:S(2)}) copy-start(f32[8,32,32]{2,1,0:T(8,128)} %table_ref.1) | copy-start | bytes 98308

commit v2 on v1

--- a/solution.py
+++ b/solution.py
@@ -175,12 +175,15 @@
 
 
 PLANES = 4
+SHARED_CUTS = 2
 MESH_IDS = pl.DeviceIdType.MESH
 
 
 def block_kernel(
     cuts,
-    planes_ref,
+    signal_ref,
+    bases_ref,
+    base_table_ref,
     taps_ref,
     gain_ref,
     shift_ref,
@@ -190,11 +193,12 @@
     k_ref,
     v_ref,
     table_ref,
-    key_codes_ref,
-    query_codes_ref,
+    buckets_ref,
     out_ref,
     tokens_ref,
     mixed_ref,
+    raw,
+    spread,
     cells,
     taps,
     sums,
@@ -266,8 +270,8 @@
         )
 
     loads = [
-        pltpu.make_async_copy(planes_ref, cells.at[0, 2:6], load_sem.at[0]),
         pltpu.make_async_copy(taps_ref, taps.at[0], load_sem.at[1]),
+        pltpu.make_async_copy(signal_ref, raw, load_sem.at[0]),
         pltpu.make_async_copy(proj_ref, proj, load_sem.at[2]),
         pltpu.make_async_copy(q_ref, q_w, load_sem.at[3]),
         pltpu.make_async_copy(k_ref, kv_w.at[:, 0:128], load_sem.at[4]),
@@ -277,7 +281,10 @@
     for load in loads:
         load.start()
 
-    codes[z] = key_codes_ref[...]
+    kinds = lax.broadcasted_iota(jnp.int32, codes.shape[1:], 0)
+    own_codes = (kinds == buckets_ref[...]).astype(jnp.float32)
+    codes[z] = own_codes.astype(jnp.bfloat16)
+    query_codes = jnp.transpose(own_codes).astype(jnp.bfloat16)
     halo[...] = jnp.zeros_like(halo)
 
     barrier = pltpu.get_barrier_semaphore()
@@ -286,29 +293,25 @@
         partners += [(place, ring[step]), (across, ring[step])]
     for partner in partners:
         pl.semaphore_signal(barrier, inc=1, device_id=partner, device_id_type=MESH_IDS)
-    loads[0].wait()
     pl.semaphore_wait(barrier, len(partners))
 
     rows = cells.shape[2]
-    to_left = copy(
-        cells.at[0, 2:4, 0:16], halo.at[1], halo_send.at[0], halo_recv.at[1], (place, z - 1)
-    )
-    to_right = copy(
-        cells.at[0, 4:6, rows - 16 : rows],
-        halo.at[0],
-        halo_send.at[1],
-        halo_recv.at[0],
-        (place, z + 1),
-    )
-    pl.when(z > 0)(to_left.start)
-    pl.when(z < depth - 1)(to_right.start)
-
     half = (taps.shape[2] // 16 + 1) // 2 * 16
     halves = (slice(0, half), slice(half, taps.shape[2]))
 
     def by_parity(act):
         for parity in (0, 1):
             pl.when(z % 2 == parity)(functools.partial(act, halves[parity], halves[1 - parity]))
+
+    def each_across(i, act):
+        if i < SHARED_CUTS:
+            by_parity(lambda mine, other: act(taps_across(i, mine)))
+        else:
+            act(taps_across(i, slice(0, taps.shape[2])))
+
+    def each_pass(i, act, received):
+        if i < SHARED_CUTS:
+            by_parity(lambda mine, other: act(taps_pass(i, other if received else mine)))
 
     def own_to_x(i):
         part = cells.at[0, 2:6, :, cuts[i]]
@@ -347,12 +350,39 @@
         )
 
     number = len(cuts)
+    loads[0].wait()
     for i in range(number):
+        each_across(i, lambda item: item.start())
+    base_kinds = lax.broadcasted_iota(jnp.int32, (8, raw.shape[0]), 0)
+    base_codes = jnp.transpose((base_kinds == bases_ref[...]).astype(jnp.float32))
+    base_codes = base_codes[:, 0:4].astype(jnp.bfloat16)
+    loads[1].wait()
+    for i in range(number):
+        cut = cuts[i]
+        embedded = raw[:, cut].astype(jnp.float32) + jnp.dot(
+            base_codes, base_table_ref[:, cut], preferred_element_type=jnp.float32
+        )
+        for start in range(cut.start, cut.stop, 128):
+            spread[start // 128] = embedded[:, start - cut.start : start - cut.start + 128]
+            for plane in range(PLANES):
+                cells[0, 2 + plane, :, start : start + 128] = spread[
+                    start // 128, pl.ds(plane, rows, stride=PLANES), :
+                ].astype(jnp.bfloat16)
         own_to_x(i).start()
-        if i == 0:
-            loads[1].wait()
-        by_parity(lambda mine, other: taps_across(i, mine).start())
         own_to_core(i).start()
+
+    to_left = copy(
+        cells.at[0, 2:4, 0:16], halo.at[1], halo_send.at[0], halo_recv.at[1], (place, z - 1)
+    )
+    to_right = copy(
+        cells.at[0, 4:6, rows - 16 : rows],
+        halo.at[0],
+        halo_send.at[1],
+        halo_recv.at[0],
+        (place, z + 1),
+    )
+    pl.when(z > 0)(to_left.start)
+    pl.when(z < depth - 1)(to_right.start)
 
     code_copies = [
         copy(codes.at[z], codes.at[z], code_send.at[s], code_recv.at[s], (place, ring[s]))
@@ -393,7 +423,7 @@
             piece = rest.astype(jnp.bfloat16)
             rest = rest - piece.astype(jnp.float32)
             of_query = jnp.dot(
-                query_codes_ref[...], piece, preferred_element_type=jnp.float32
+                query_codes, piece, preferred_element_type=jnp.float32
             ).astype(jnp.bfloat16)
             for s in range(depth):
                 block = jnp.dot(of_query, codes[s], preferred_element_type=jnp.float32)
@@ -408,13 +438,13 @@
     for item in edge_copies:
         item.wait_recv()
 
-    def convolve(i):
+    def convolve(i, first, last, sides, shifts):
         cut = cuts[i]
 
         def one_window(slot, carry):
             fringe = edges[slot, :, cut].astype(jnp.float32)
             line = lax.broadcasted_iota(jnp.int32, (rows, 1), 0)
-            for target, source, edge_row in ((0, 4, 0), (1, 5, 1), (6, 2, 2), (7, 3, 3)):
+            for target, source, edge_row in shifts:
                 values = cells[slot, source, :, cut].astype(jnp.float32)
                 if target < 2:
                     moved, end = pltpu.roll(values, 1, 0), 0
@@ -423,7 +453,7 @@
                 cells[slot, target, :, cut] = jnp.where(
                     line == end, fringe[edge_row : edge_row + 1], moved
                 ).astype(jnp.bfloat16)
-            for side in range(2):
+            for side in sides:
                 total = None
                 for t in range(taps.shape[1]):
                     part = cells[slot, t : t + PLANES, :, cut].reshape(PLANES * rows, -1)
@@ -440,23 +470,28 @@
                     sums[slot, side] += total
             return carry
 
-        lax.fori_loop(0, 4, one_window, 0)
+        lax.fori_loop(first, last, one_window, 0)
 
     def arrive(i):
+        pass_on(i).wait_recv()
+        each_pass(i, lambda item: item.wait_recv(), True)
+
+    shifted = ((0, 4, 0), (1, 5, 1), (6, 2, 2), (7, 3, 3))
+    for i in range(number):
         own_to_core(i).wait_recv()
-        pass_on(i).wait_recv()
-        by_parity(lambda mine, other: taps_pass(i, other).wait_recv())
-
+        convolve(i, 0, 2, (0,), shifted)
     for i in range(number):
         own_to_x(i).wait_recv()
         pass_on(i).start()
-        by_parity(lambda mine, other: taps_across(i, mine).wait_recv())
-        by_parity(lambda mine, other: taps_pass(i, mine).start())
+        each_across(i, lambda item: item.wait_recv())
+        each_pass(i, lambda item: item.start(), False)
         if i:
             arrive(i - 1)
-            convolve(i - 1)
+            convolve(i - 1, 2, 4, (0, 1), shifted)
+            convolve(i - 1, 0, 2, (1,), ())
     arrive(number - 1)
-    convolve(number - 1)
+    convolve(number - 1, 2, 4, (0, 1), shifted)
+    convolve(number - 1, 0, 2, (1,), ())
 
     local = 4 * PLANES * rows
     line = lax.broadcasted_iota(jnp.int32, (8, 1), 0)
@@ -577,8 +612,8 @@
         own_to_x(i).wait_send()
         own_to_core(i).wait_send()
         pass_on(i).wait_send()
-        by_parity(lambda mine, other: taps_across(i, mine).wait_send())
-        by_parity(lambda mine, other: taps_pass(i, mine).wait_send())
+        each_across(i, lambda item: item.wait_send())
+        each_pass(i, lambda item: item.wait_send(), False)
     for item in code_copies + edge_copies + stat_copies + pool_copies + kv_copies:
         item.wait_send()
 
@@ -606,18 +641,7 @@
     share = conv_weight.shape[2]
     heads, classes = bias_table.shape[:2]
     model = proj_weight.shape[1]
-    base_onehot = (bases[0][:, None] == jnp.arange(4, dtype=jnp.int32)[None, :]).astype(
-        jnp.bfloat16
-    )
-    embedded = (
-        signal[0].astype(jnp.float32)
-        + jnp.dot(base_onehot, base_table, preferred_element_type=jnp.float32)
-    ).astype(jnp.bfloat16)
-    planes = jnp.transpose(embedded.reshape(rows, PLANES, channels), (1, 0, 2))
     taps = jnp.transpose(conv_weight, (0, 2, 1))
-    kinds = jnp.arange(classes, dtype=jnp.int32)
-    query_codes = (buckets[0][:, None] == kinds[None, :]).astype(jnp.bfloat16)
-    key_codes = (kinds[:, None] == buckets[0][None, :]).astype(jnp.bfloat16)
     cuts = tuple(
         slice(start, min(start + 256, channels)) for start in range(0, channels, 256)
     )
@@ -631,6 +655,8 @@
         out_shape=[jax.ShapeDtypeStruct((rows, model), narrow)] * 2,
         in_specs=[
             anywhere,
+            vmem,
+            vmem,
             anywhere,
             vmem,
             vmem,
@@ -641,11 +667,12 @@
             anywhere,
             vmem,
             vmem,
-            vmem,
             anywhere,
         ],
         out_specs=[vmem, vmem],
         scratch_shapes=[
+            pltpu.VMEM((positions, channels), narrow),
+            pltpu.VMEM((channels // 128, positions, 128), wide),
             pltpu.VMEM((4, PLANES + width - 1, rows, channels), narrow),
             pltpu.VMEM((2, width, share, channels), narrow),
             pltpu.VMEM((4, 2, positions, share), wide),
@@ -693,7 +720,9 @@
             flops=12_000_000_000, bytes_accessed=20_000_000, transcendentals=4_000_000
         ),
     )(
-        planes,
+        signal[0],
+        bases,
+        base_table,
         taps,
         batch_norm_gain.reshape(devices, 1, share),
         norm_bias.reshape(devices, 1, share),
@@ -703,8 +732,7 @@
         k_weight,
         v_weight,
         bias_table,
-        key_codes,
-        query_codes,
+        buckets,
         out_weight,
     )
     return (tokens[None], mixed[None])

time: 108 us -> 106 us (0.981)
  matrix products: 3.08 us -> 0 us
  local copies, waits for them, and re-layouts: 6.51 us -> 8.7 us
  Pallas kernels: 97.3 us -> 95.8 us
    unnamed x18 -> x14, local copies, waits for them, and re-layouts: 2.23 us -> 6.42 us
    reshape x2 -> x0, local copies, waits for them, and re-layouts: 4.09 us -> none  [fused_shards(): planes = jnp.transpose(embedded.reshape(rows, PLANES, channels), (1, 0, 2))]
    dot_general x1 -> x0, matrix products: 3.08 us -> none  [fused_shards(): jnp.dot(base_onehot, base_table, preferred_element_type=jnp.float32)]
    pallas_call x1, Pallas kernels: 97.3 us -> 95.8 us  [fused_shards(): pl.pallas_call(functools.partial(block_kernel, cuts), out_shape=[jax.Shap...]
where the time goes in v2:
time: 106 us; the launch traced here: 105 us
  Pallas kernels  95.8 us (90%)
  local copies, waits for them, and re-layouts  8.7 us (8%)
    pallas_call x1, Pallas kernels, fused_shards(): pl.pallas_call(functools.partial(block_kernel, cuts), out_shape=[jax.Shap...  95.8 us
    unnamed x14, local copies, waits for them, and re-layouts  6.42 us

profile of v2, /device:TPU:0, one launch (start us, length us, event | category | flops | bytes accessed | tf_op | source)
XLA Modules:
  0.0 105.1 jit_solution(2721660017498494545)
XLA Ops:
  0.6 0.7 broadcast_in_dim.9.attn_gain_ref
  1.3 0.8 reshape.10.gain_ref
  2.1 0.8 reshape.11.shift_ref
  2.9 0.0 copy-start
  2.9 1.0 copy-done
  3.9 0.0 copy-start.1
  3.9 1.0 copy-done.1
  4.9 0.0 copy-start.2
  4.9 0.9 copy-done.2
  5.8 0.0 copy-start.3
  5.8 0.7 copy-done.3
  6.5 0.0 copy-start.4
  6.5 0.7 copy-done.4
  7.2 0.0 copy-start.5
  7.2 0.7 copy-done.5
  7.9 95.8 %shard_map.149 = (bf16[128,1536]{1,0:T(8,128)(2,1)S(1)}, bf16[128,1536]{1,0:T(8,128)(2,1)S(1)}) custom-call(bf16[512,1408]{1,0:T(8,128)(2,1)} %bitcast.7, s32[1,512]{1,0:T(1,128)S(1)} %copy-done.4, bf16[4,1408]{1,0:T(4,128)(2,1)S(1)} %copy-done.3, bf16[5,176,1408]{2,1,0:T(8,128)(2,1)} %bitcast.6, f32[8,1,176]{2,1,0:T(1,128)S(1)} %reshape.10.gain_ref, ...), custom_call_target="tpu_custom_call" | custom-call | flops 12000000000 | bytes 20000000 | tf_op jit(solution)/shard_map/pallas_call | solution.py:653
  103.6 0.7 copy.18
  104.4 0.7 copy.19
Async XLA Ops:
  2.9 1.0 copy-start
  3.9 1.0 copy-start.1
  4.9 0.9 copy-start.2
  5.8 0.7 copy-start.3
  6.5 0.7 copy-start.4
  7.2 0.7 copy-start.5
